TPU v7x, 32 devices: a whole 2x2x4 slice. The times are simulated.
32 devices in a mesh: gx: 4 (over y, core), gy: 8 (over z, x).
Axes of the slice: x: 2, y: 2, z: 4, core: 2. Of those that a mesh axis runs over, the one named last changes fastest.
Arguments:
- velocity: float32 [3, 32, 64, 512], P(None, 'gx', 'gy'), may hold values from -6 to 6
- stress: float32 [6, 32, 64, 512], P(None, 'gx', 'gy'), may hold values from -6 to 6
- lame_lambda: float32 [32, 64, 512], P('gx', 'gy'), may hold values from 0.5 to 5
- lame_mu: float32 [32, 64, 512], P('gx', 'gy'), may hold values from 0.5 to 5
- node_mass: float32 [32, 64, 512], P('gx', 'gy'), may hold values from 0.5 to 2
- displacement: float32 [3, 32, 64, 512], P(None, 'gx', 'gy'), may hold values from -0.75 to 0.75
- seg_elem: int32 [65536], P(('gx', 'gy')), may hold values from 0 to 32767
- seg_bucket: int32 [65536, 1], P(('gx', 'gy')), may hold values from 0 to 31; in each aligned block of 2048 rows (0 to 2047, 2048 to 4095, ...) at most 128 rows name the same one
- slave_points: float32 [3, 16384], P(None, ('gx', 'gy')), may hold values from 0.8 to 1.2
- candidates: int32 [4, 16384], P(None, ('gx', 'gy')), may hold values from 0 to 4095
Outputs:
- new_stress: float32 [6, 32, 64, 512], P(None, 'gx', 'gy')
- acceleration: float32 [3, 32, 64, 512], P(None, 'gx', 'gy')
- slave_force: float32 [3, 16384], P(None, ('gx', 'gy'))
Inputs may be any that keep to these rules, and one draw needn't show every extreme that they name: `seg_bucket`: in the rows of one device no bucket is named more than 128 times. `candidates`: A slot index into the 32 x 128 segment slots of the slave's own bucket, source device major; a slot holding no segment contributes nothing.
All inputs are finite; a program needn't handle non-finite values.
Results may differ from a plain program's by a relative error of at most 0.0003.
Values sent between devices are 32-bit elements; how exact they have to be, the bound alone decides.
A program may use at most 128 MiB of HBM per device.

v0:
```python
import jax
import jax.numpy as jnp
from jax import lax
from jax.sharding import PartitionSpec as P

time_step = 0.1
penalty = 10.0


def shifted(array, axis, by):
    size = lax.axis_size(axis)
    pairs = [(i, i + by) for i in range(size) if 0 <= i + by < size]
    return lax.ppermute(array, axis, pairs)


def element_pass(extended, stress, lame_lambda, lame_mu):
    size_x = extended.shape[1] - 1
    size_y = extended.shape[2] - 1
    size_z = extended.shape[3] - 1
    nodal = extended[0:3]

    def corner_vel(side_x, side_y, side_z):
        return nodal[
            :, side_x : side_x + size_x, side_y : side_y + size_y, side_z : side_z + size_z
        ]

    grad_x = 0.25 * sum((corner_vel(1, p, q) - corner_vel(0, p, q) for p in (0, 1) for q in (0, 1)))
    grad_y = 0.25 * sum((corner_vel(p, 1, q) - corner_vel(p, 0, q) for p in (0, 1) for q in (0, 1)))
    grad_z = 0.25 * sum((corner_vel(p, q, 1) - corner_vel(p, q, 0) for p in (0, 1) for q in (0, 1)))
    rate_xx = grad_x[0]
    rate_yy = grad_y[1]
    rate_zz = grad_z[2]
    rate_yz = 0.5 * (grad_z[1] + grad_y[2])
    rate_xz = 0.5 * (grad_z[0] + grad_x[2])
    rate_xy = 0.5 * (grad_y[0] + grad_x[1])
    volume_rate = rate_xx + rate_yy + rate_zz
    stress_xx = stress[0] + time_step * (lame_lambda * volume_rate + 2.0 * lame_mu * rate_xx)
    stress_yy = stress[1] + time_step * (lame_lambda * volume_rate + 2.0 * lame_mu * rate_yy)
    stress_zz = stress[2] + time_step * (lame_lambda * volume_rate + 2.0 * lame_mu * rate_zz)
    stress_yz = stress[3] + time_step * 2.0 * lame_mu * rate_yz
    stress_xz = stress[4] + time_step * 2.0 * lame_mu * rate_xz
    stress_xy = stress[5] + time_step * 2.0 * lame_mu * rate_xy
    new_stress = jnp.stack([stress_xx, stress_yy, stress_zz, stress_yz, stress_xz, stress_xy])
    tensor = (
        (stress_xx, stress_xy, stress_xz),
        (stress_xy, stress_yy, stress_yz),
        (stress_xz, stress_yz, stress_zz),
    )
    forces = jnp.zeros((3, size_x + 1, size_y + 1, size_z + 1), extended.dtype)
    for side_x in (0, 1):
        for side_y in (0, 1):
            for side_z in (0, 1):
                sign_x = 2.0 * side_x - 1.0
                sign_y = 2.0 * side_y - 1.0
                sign_z = 2.0 * side_z - 1.0
                part = jnp.stack(
                    [
                        -0.25
                        * (
                            sign_x * tensor[row][0]
                            + sign_y * tensor[row][1]
                            + sign_z * tensor[row][2]
                        )
                        for row in range(3)
                    ]
                )
                forces = forces + jnp.pad(
                    part, ((0, 0), (side_x, 1 - side_x), (side_y, 1 - side_y), (side_z, 1 - side_z))
                )
    return (new_stress, forces)


def seg_geometry(corners):
    low_low = corners[0:3]
    high_low = corners[3:6]
    high_high = corners[6:9]
    low_high = corners[9:12]
    centre = 0.25 * (low_low + high_low + high_high + low_high)
    first = high_high - low_low
    second = low_high - high_low
    area = 0.5 * jnp.stack(
        [
            first[1] * second[2] - first[2] * second[1],
            first[2] * second[0] - first[0] * second[2],
            first[0] * second[1] - first[1] * second[0],
        ]
    )
    return (centre, area)


def slot_rank(bucket, devices):
    onehot = (bucket[:, None] == jnp.arange(devices, dtype=jnp.int32)[None, :]).astype(jnp.int32)
    running = jnp.cumsum(onehot, axis=0)
    return jnp.sum(running * onehot, axis=1) - 1


def per_device(
    velocity,
    stress,
    lame_lambda,
    lame_mu,
    node_mass,
    displacement,
    seg_elem,
    seg_bucket,
    slave_points,
    candidates,
):
    count_x = lax.axis_size("gx")
    count_y = lax.axis_size("gy")
    devices = count_x * count_y
    size_x = velocity.shape[1]
    size_y = velocity.shape[2]
    size_z = velocity.shape[3]
    seg_count = seg_elem.shape[0]
    capacity = 2 * seg_count // devices
    slots = devices * capacity
    own = jnp.concatenate([velocity, displacement], 0)
    ghost_x = shifted(own[:, :1], "gx", -1)
    extended = jnp.concatenate([own, ghost_x], 1)
    ghost_y = shifted(extended[:, :, :1], "gy", -1)
    extended = jnp.concatenate([extended, ghost_y], 2)
    extended = jnp.pad(extended, ((0, 0), (0, 0), (0, 0), (0, 1)))
    new_stress, forces = element_pass(extended, stress, lame_lambda, lame_mu)
    bucket = seg_bucket[:, 0]
    ranks = slot_rank(bucket, devices)
    target = bucket * capacity + ranks
    cell_i = seg_elem // (size_y * size_z)
    cell_j = seg_elem // size_z % size_y
    cell_k = seg_elem % size_z
    flat_disp = extended[3:6].reshape(3, -1)
    offsets = ((0, 0), (1, 0), (1, 1), (0, 1))
    indices = []
    pieces = []
    for off_a, off_b in offsets:
        index = ((cell_i + off_a) * (size_y + 1) + cell_j + off_b) * (size_z + 1) + cell_k + 1
        indices.append(index)
        shift_vec = jnp.array([off_a, off_b, 1.0], jnp.float32)[:, None]
        pieces.append(flat_disp[:, index] + shift_vec)
    corners = jnp.concatenate(pieces, 0)
    centre_own, area_own = seg_geometry(corners)
    payload = jnp.concatenate([centre_own, area_own], 0)
    width = payload.shape[0]
    outgoing = jnp.zeros((width, slots), jnp.float32).at[:, target].set(payload)
    arrived = lax.all_to_all(
        outgoing.reshape(width, devices, capacity),
        ("gx", "gy"),
        split_axis=1,
        concat_axis=1,
        tiled=True,
    )
    arrived = arrived.reshape(width, slots)
    centre = arrived[0:3]
    area = arrived[3:6]
    flat_candidates = candidates.reshape(-1)
    table = jnp.concatenate([centre, area], 0)
    near = table[:, flat_candidates].reshape(6, candidates.shape[0], candidates.shape[1])
    near_centre = near[0:3]
    near_area = near[3:6]
    gap = jnp.sum(near_area * (slave_points[:, None, :] - near_centre), axis=0)
    push = penalty * jnp.maximum(-gap, 0.0)[None] * near_area
    slave_force = jnp.sum(push, axis=1)
    reaction = jnp.zeros((3, slots), jnp.float32).at[:, flat_candidates].add(-push.reshape(3, -1))
    returned = lax.all_to_all(
        reaction.reshape(3, devices, capacity),
        ("gx", "gy"),
        split_axis=1,
        concat_axis=1,
        tiled=True,
    )
    returned = returned.reshape(3, slots)
    quarter = 0.25 * returned[:, target]
    flat_forces = forces.reshape(3, -1)
    for index in indices:
        flat_forces = flat_forces.at[:, index].add(quarter)
    forces = flat_forces.reshape(forces.shape)[:, :, :, :size_z]
    upper_y = shifted(forces[:, :, size_y : size_y + 1], "gy", 1)
    forces = forces[:, :, :size_y] + jnp.pad(upper_y, ((0, 0), (0, 0), (0, size_y - 1), (0, 0)))
    upper_x = shifted(forces[:, size_x : size_x + 1], "gx", 1)
    forces = forces[:, :size_x] + jnp.pad(upper_x, ((0, 0), (0, size_x - 1), (0, 0), (0, 0)))
    acceleration = forces / node_mass[None]
    return (new_stress, acceleration, slave_force)


def solution(mesh):
    return jax.shard_map(
        per_device,
        mesh=mesh,
        in_specs=(
            P(None, "gx", "gy", None),
            P(None, "gx", "gy", None),
            P("gx", "gy", None),
            P("gx", "gy", None),
            P("gx", "gy", None),
            P(None, "gx", "gy", None),
            P(("gx", "gy")),
            P(("gx", "gy"), None),
            P(None, ("gx", "gy")),
            P(None, ("gx", "gy")),
        ),
        out_specs=(P(None, "gx", "gy", None), P(None, "gx", "gy", None), P(None, ("gx", "gy"))),
        check_vma=False,
    )
```

profile of v0, /device:TPU:12, one launch (start us, length us, event | category | flops | bytes accessed | tf_op | source)
XLA Modules:
  0.0 286.3 jit_solution(2993142969272704066)
XLA Ops:
  0.7 1.0 constant_dynamic-update-slice_fusion.1
  1.7 1.0 constant_dynamic-update-slice_fusion
  2.7 1.9 collective-permute-start
  4.8 9.1 %reduce-window.6 = s32[32,16,128]{2,1,0:T(8,128)S(1)} reduce-window(s32[32,16,128]{2,1,0:T(8,128)S(1)} %fusion.32, s32[]{:T(128)} %constant.89.clone.1), window={size=1x1x128 pad=0_0x0_0x127_0}, to_apply=%region_0.1 | reduce-window | flops 8323072 | bytes 524292 | tf_op jit(solution)/shard_map/reduce-window
  14.7 0.6 broadcast_clamp_fusion.4
  15.5 3.3 %collective-permute-start.1 = (f32[6,9,1,512]{3,2,1,0:T(1,128)S(1)}, f32[6,9,1,512]{3,2,1,0:T(1,128)S(1)}, u32[]{:S(2)}, u32[]{:S(2)}) collective-permute-start(f32[6,9,1,512]{3,2,1,0:T(1,128)S(1)} %pad_maximum_fusion.3), channel_id=1, source_target_pairs={{1,0},{2,1},{3,2},{4,3},{5,4},{6,5},{7,6},{9,8},{10,9},{11,10},{12... | collective-permute-start | bytes 331784 | tf_op jit(solution)/shard_map/ppermute | solution.py:13
  18.8 0.9 copy.67
  19.6 3.2 %collective-permute-done.1 = f32[6,9,1,512]{3,2,1,0:T(1,128)S(1)} collective-permute-done((f32[6,9,1,512]{3,2,1,0:T(1,128)S(1)}, f32[6,9,1,512]{3,2,1,0:T(1,128)S(1)}, u32[]{:S(2)}, u32[]{:S(2)}) %collective-permute-start.1) | collective-permute-done | bytes 110624 | tf_op jit(solution)/shard_map/ppermute | solution.py:13
  23.2 0.9 copy-done.1
  24.5 0.9 add_multiply_fusion.1
  25.5 0.7 reshape.123
  26.4 1.9 multiply_bitcast_fusion.23
  28.4 1.1 multiply_bitcast_fusion.20
  29.5 1.1 multiply_bitcast_fusion.19
  30.6 1.0 multiply_bitcast_fusion.18
  31.7 10.6 %copy.56 = f32[3,41553]{0,1:T(8,128)} copy(f32[3,41553]{1,0:T(4,128)S(1)} %reshape.123) | data formatting | bytes 997272 | tf_op jit(solution)/shard_map/reshape | solution.py:131
  42.3 12.5 %gather_fusion.3 = f32[2048,3]{1,0:T(8,128)S(1)} fusion(f32[3,41553]{0,1:T(8,128)} %copy.56, s32[2048]{0:T(1024)S(1)} %get-tuple-element.69), kind=kCustom, calls=%fused_computation.3 | custom fusion | bytes 57344 | tf_op jit(solution)/shard_map/gather | solution.py:139
  55.1 12.5 %gather_fusion.2 = f32[2048,3]{1,0:T(8,128)S(1)} fusion(f32[3,41553]{0,1:T(8,128)} %copy.56, s32[2048]{0:T(1024)S(1)} %get-tuple-element.67), kind=kCustom, calls=%fused_computation.2 | custom fusion | bytes 57344 | tf_op jit(solution)/shard_map/gather | solution.py:139
  68.1 12.5 %gather_fusion.1 = f32[2048,3]{1,0:T(8,128)S(1)} fusion(f32[3,41553]{0,1:T(8,128)} %copy.56, s32[2048]{0:T(1024)S(1)} %get-tuple-element.9), kind=kCustom, calls=%fused_computation.1 | custom fusion | bytes 57344 | tf_op jit(solution)/shard_map/gather | solution.py:139
  80.6 12.5 %gather_fusion = f32[2048,3]{1,0:T(8,128)S(1)} fusion(f32[3,41553]{0,1:T(8,128)} %copy.56, s32[2048]{0:T(1024)S(1)} %get-tuple-element.71), kind=kCustom, calls=%fused_computation | custom fusion | bytes 57344 | tf_op jit(solution)/shard_map/gather | solution.py:139
  94.4 6.2 %scatter_custom_fusion = f32[6,4096]{0,1:T(8,128)S(1)} fusion(s32[2048]{0:T(1024)} %bitcast.195, f32[2048,6]{1,0:T(8,128)S(1)} %copy.64, f32[]{:T(128)} %constant.80.clone.1), kind=kCustom, calls=%fused_computation.63 | custom fusion | bytes 98816 | tf_op jit(solution)/shard_map/scatter | solution.py:144
  100.7 1.3 copy.65
  102.0 5.9 %all-to-all-start = ((f32[6,32,128]{2,0,1:T(8,128)}), f32[6,32,128]{2,0,1:T(8,128)S(1)}, u32[]{:S(2)}, u32[]{:S(2)}) async-start(f32[6,32,128]{2,0,1:T(8,128)} %copy.65), calls=%async_computation | async-start | bytes 262144 | tf_op jit(solution)/shard_map/all_to_all | solution.py:145
  108.0 5.1 %fusion = f32[3,9,9,513]{3,2,1,0:T(8,128)} fusion(f32[1,8,8,512]{3,2,1,0:T(8,128)} %get-tuple-element.50, f32[1,8,8,512]{3,2,1,0:T(8,128)} %get-tuple-element.44, f32[1,8,8,512]{3,2,1,0:T(8,128)S(1)} %copy-done.9, f32[1,8,8,512]{3,2,1,0:T(8,128)} %get-tuple-element.49, f32[1,8,8,512]{3,2,1,0:T(8,128)} %get-tuple-element.43, ...), kind=kLoop, calls=%fused_computation.19 | loop fusion | flops 14086467 | bytes 3644364 | tf_op jit(solution)/shard_map/add | solution.py:67
  113.1 0.7 bitcast_dynamic-update-slice_fusion.2
  114.0 0.6 copy.66
  114.6 5.5 %gather_fusion.4 = f32[2048,6]{1,0:T(8,128)S(1)} fusion(f32[6,4096]{0,1:T(8,128)S(1)} %copy.66, s32[2048]{0:T(1024)S(1)} %get-tuple-element.73), kind=kCustom, calls=%fused_computation.4 | custom fusion | bytes 106496 | tf_op jit(solution)/shard_map/gather | solution.py:157
  120.1 2.3 fusion.54
  122.4 13.1 %scatter_custom_fusion.1 = f32[3,4096]{0,1:T(8,128)S(1)} fusion(s32[2048]{0:T(1024)} %bitcast.199, f32[]{:T(128)} %constant.80.clone.1, f32[2048]{0:T(1024)S(1)} %maximum_multiply_fusion.1, f32[6,2048]{0,1:T(8,128)S(1)} %bitcast.184), kind=kCustom, calls=%fused_computation.58 | custom fusion | flops 18432 | bytes 107008 | tf_op jit(solution)/shard_map/scatter-add | solution.py:163
  135.5 1.2 copy.68
  136.8 5.6 %all-to-all-start.1 = ((f32[3,32,128]{2,0,1:T(4,128)}), f32[3,32,128]{2,0,1:T(4,128)S(1)}, u32[]{:S(2)}, u32[]{:S(2)}) async-start(f32[3,32,128]{2,0,1:T(4,128)} %copy.68), calls=%async_computation.1 | async-start | bytes 131072 | tf_op jit(solution)/shard_map/all_to_all | solution.py:164
  142.4 0.7 bitcast_dynamic-update-slice_fusion.1
  143.1 1.9 reshape.120
  145.0 10.6 %copy.70 = f32[3,41553]{0,1:T(8,128)} copy(f32[3,41553]{1,0:T(4,128)S(1)} %reshape.120) | data formatting | bytes 997272 | tf_op jit(solution)/shard_map/reshape | solution.py:173
  155.7 0.6 copy.69
  156.3 5.5 %gather_fusion.5 = f32[2048,3]{1,0:T(8,128)S(1)} fusion(f32[3,4096]{0,1:T(8,128)S(1)} %bitcast.188, s32[2048]{0:T(1024)S(1)} %broadcast_clamp_fusion), kind=kCustom, calls=%fused_computation.5 | custom fusion | bytes 57344 | tf_op jit(solution)/shard_map/gather | solution.py:172
  161.8 24.6 %scatter_custom_fusion.2 = f32[3,41553]{0,1:T(8,128)} fusion(f32[3,41553]{0,1:T(8,128)} %copy.70, s32[2048]{0:T(1024)} %get-tuple-element.72, f32[2048,3]{1,0:T(8,128)S(1)} %gather_fusion.5, f32[]{:T(128)} %constant.81.clone.1), kind=kCustom, calls=%fused_computation.70 | custom fusion | flops 12288 | bytes 523724 | tf_op jit(solution)/shard_map/scatter-add | solution.py:175
  186.4 24.6 %scatter_custom_fusion.3 = f32[3,41553]{0,1:T(8,128)} fusion(f32[3,41553]{0,1:T(8,128)} %scatter_custom_fusion.2, s32[2048]{0:T(1024)} %get-tuple-element.10, f32[2048,3]{1,0:T(8,128)S(1)} %gather_fusion.5, f32[]{:T(128)} %constant.81.clone.1), kind=kCustom, calls=%fused_computation.68 | custom fusion | flops 12288 | bytes 523724 | tf_op jit(solution)/shard_map/scatter-add | solution.py:175
  211.0 24.6 %scatter_custom_fusion.4 = f32[3,41553]{0,1:T(8,128)} fusion(f32[3,41553]{0,1:T(8,128)} %scatter_custom_fusion.3, s32[2048]{0:T(1024)} %get-tuple-element.68, f32[2048,3]{1,0:T(8,128)S(1)} %gather_fusion.5, f32[]{:T(128)} %constant.81.clone.1), kind=kCustom, calls=%fused_computation.66 | custom fusion | flops 12288 | bytes 523724 | tf_op jit(solution)/shard_map/scatter-add | solution.py:175
  235.7 24.6 %scatter_custom_fusion.5 = f32[3,41553]{0,1:T(8,128)} fusion(f32[3,41553]{0,1:T(8,128)} %scatter_custom_fusion.4, s32[2048]{0:T(1024)} %get-tuple-element.70, f32[2048,3]{1,0:T(8,128)S(1)} %gather_fusion.5, f32[]{:T(128)} %constant.81.clone.1), kind=kCustom, calls=%fused_computation.72 | custom fusion | flops 12288 | bytes 523724 | tf_op jit(solution)/shard_map/scatter-add | solution.py:175
  260.3 12.0 %copy.71 = f32[3,41553]{1,0:T(4,128)S(1)} copy(f32[3,41553]{0,1:T(8,128)} %scatter_custom_fusion.5) | data formatting | bytes 997272 | tf_op jit(solution)/shard_map/scatter-add | solution.py:175
  272.9 3.5 %collective-permute-start.2 = (f32[3,9,1,512]{3,2,1,0:T(1,128)S(1)}, f32[3,9,1,512]{3,2,1,0:T(1,128)S(1)}, u32[]{:S(2)}, u32[]{:S(2)}) collective-permute-start(f32[3,9,1,512]{3,2,1,0:T(1,128)S(1)} %slice.256), channel_id=1, source_target_pairs={{0,1},{1,2},{2,3},{3,4},{4,5},{5,6},{6,7},{8,9},{9,10},{10,11},{11... | collective-permute-start | bytes 165896 | tf_op jit(solution)/shard_map/ppermute | solution.py:13
  276.4 0.7 bitcast_dynamic-update-slice_fusion
  277.1 2.9 %collective-permute-done.2 = f32[3,9,1,512]{3,2,1,0:T(1,128)S(1)} collective-permute-done((f32[3,9,1,512]{3,2,1,0:T(1,128)S(1)}, f32[3,9,1,512]{3,2,1,0:T(1,128)S(1)}, u32[]{:S(2)}, u32[]{:S(2)}) %collective-permute-start.2) | collective-permute-done | bytes 55328 | tf_op jit(solution)/shard_map/ppermute | solution.py:13
  280.1 1.9 collective-permute-start.3
  282.4 0.7 copy.72
  283.1 2.4 collective-permute-done.3
  285.5 0.8 fusion.29
  (88 shorter events, 5.4 us)
Async XLA Ops:
  0.6 4.0 %copy-start.19 = (s32[4,512]{1,0:T(4,128)S(1)}, s32[4,512]{1,0:T(4,128)}, u32[]{:S(2)}) copy-start(s32[4,512]{1,0:T(4,128)} %param.23) | copy-start | bytes 24580
  0.6 4.1 %copy-start.14 = (s32[2048,1]{0,1:T(1,128)S(1)}, s32[2048,1]{0,1:T(1,128)}, u32[]{:S(2)}) copy-start(s32[2048,1]{0,1:T(1,128)} %param.21) | copy-start | bytes 24580
  2.7 12.7 %collective-permute-start = (f32[6,1,8,512]{3,2,1,0:T(8,128)S(1)}, f32[6,1,8,512]{3,2,1,0:T(8,128)S(1)}, u32[]{:S(2)}, u32[]{:S(2)}) collective-permute-start(f32[6,1,8,512]{3,2,1,0:T(8,128)S(1)} %slice.231), channel_id=1, source_target_pairs={{8,0},{16,8},{24,16},{9,1},{17,9},{25,17},{10,2},{18,10},{26,18},{... | collective-permute-start | bytes 294920 | tf_op jit(solution)/shard_map/ppermute | solution.py:13
  4.7 10.0 %copy-start.16 = (s32[2048,1]{0,1:T(1,128)}, s32[2048,1]{0,1:T(1,128)S(1)}, u32[]{:S(2)}) copy-start(s32[2048,1]{0,1:T(1,128)S(1)} %compare_select_fusion.1) | copy-start | bytes 24580
  4.8 10.0 %copy-start.20 = (s32[2048]{0:T(1024)S(1)}, s32[2048]{0:T(1024)}, u32[]{:S(2)}) copy-start(s32[2048]{0:T(1024)} %param.20) | copy-start | bytes 24580
  14.0 4.8 %copy-start.18 = (f32[3,512]{1,0:T(4,128)S(1)}, f32[3,512]{1,0:T(4,128)}, u32[]{:S(2)}) copy-start(f32[3,512]{1,0:T(4,128)} %param.22) | copy-start | bytes 18436
  14.7 8.3 %copy-start.15 = (s32[2048,1]{0,1:T(1,128)}, s32[2048,1]{0,1:T(1,128)S(1)}, u32[]{:S(2)}) copy-start(s32[2048,1]{0,1:T(1,128)S(1)} %compare_select_fusion) | copy-start | bytes 24580
  15.5 7.4 %collective-permute-start.1 = (f32[6,9,1,512]{3,2,1,0:T(1,128)S(1)}, f32[6,9,1,512]{3,2,1,0:T(1,128)S(1)}, u32[]{:S(2)}, u32[]{:S(2)}) collective-permute-start(f32[6,9,1,512]{3,2,1,0:T(1,128)S(1)} %pad_maximum_fusion.3), channel_id=1, source_target_pairs={{1,0},{2,1},{3,2},{4,3},{5,4},{6,5},{7,6},{9,8},{10,9},{11,10},{12... | collective-permute-start | bytes 331784 | tf_op jit(solution)/shard_map/ppermute | solution.py:13
  23.0 1.0 copy-start.1
  25.5 0.9 copy-start.2
  25.5 1.0 copy-start.12
  26.4 2.0 copy-start.3
  31.7 10.6 %copy-start.17 = (f32[6,8,8,512]{3,2,1,0:T(8,128)}, f32[6,8,8,512]{3,2,1,0:T(8,128)S(1)}, u32[]{:S(2)}) copy-start(f32[6,8,8,512]{3,2,1,0:T(8,128)S(1)} %bitcast_dynamic-update-slice_fusion.3) | copy-start | bytes 2359300
  93.1 0.7 copy-start.21
  93.1 0.7 copy-start.22
  93.2 0.7 copy-start.23
  100.7 7.2 %copy-start.4 = (f32[1,8,8,512]{3,2,1,0:T(8,128)S(1)}, f32[1,8,8,512]{3,2,1,0:T(8,128)}, u32[]{:S(2)}) copy-start(f32[1,8,8,512]{3,2,1,0:T(8,128)} %get-tuple-element.17) | copy-start | bytes 393220
  100.7 7.2 %copy-start.5 = (f32[1,8,8,512]{3,2,1,0:T(8,128)S(1)}, f32[1,8,8,512]{3,2,1,0:T(8,128)}, u32[]{:S(2)}) copy-start(f32[1,8,8,512]{3,2,1,0:T(8,128)} %get-tuple-element.33) | copy-start | bytes 393220
  100.7 7.2 %copy-start.6 = (f32[1,8,8,512]{3,2,1,0:T(8,128)S(1)}, f32[1,8,8,512]{3,2,1,0:T(8,128)}, u32[]{:S(2)}) copy-start(f32[1,8,8,512]{3,2,1,0:T(8,128)} %get-tuple-element.34) | copy-start | bytes 393220
  100.7 7.2 %copy-start.7 = (f32[1,8,8,512]{3,2,1,0:T(8,128)S(1)}, f32[1,8,8,512]{3,2,1,0:T(8,128)}, u32[]{:S(2)}) copy-start(f32[1,8,8,512]{3,2,1,0:T(8,128)} %get-tuple-element.35) | copy-start | bytes 393220
  100.7 7.2 %copy-start.8 = (f32[1,8,8,512]{3,2,1,0:T(8,128)S(1)}, f32[1,8,8,512]{3,2,1,0:T(8,128)}, u32[]{:S(2)}) copy-start(f32[1,8,8,512]{3,2,1,0:T(8,128)} %get-tuple-element.36) | copy-start | bytes 393220
  100.7 7.2 %copy-start.9 = (f32[1,8,8,512]{3,2,1,0:T(8,128)S(1)}, f32[1,8,8,512]{3,2,1,0:T(8,128)}, u32[]{:S(2)}) copy-start(f32[1,8,8,512]{3,2,1,0:T(8,128)} %get-tuple-element.37) | copy-start | bytes 393220
  100.7 7.2 %copy-start.10 = (f32[1,8,8,512]{3,2,1,0:T(8,128)S(1)}, f32[1,8,8,512]{3,2,1,0:T(8,128)}, u32[]{:S(2)}) copy-start(f32[1,8,8,512]{3,2,1,0:T(8,128)} %get-tuple-element.38) | copy-start | bytes 393220
  100.7 7.2 %copy-start.11 = (f32[1,8,8,512]{3,2,1,0:T(8,128)S(1)}, f32[1,8,8,512]{3,2,1,0:T(8,128)}, u32[]{:S(2)}) copy-start(f32[1,8,8,512]{3,2,1,0:T(8,128)} %get-tuple-element.39) | copy-start | bytes 393220
  102.0 11.9 %all-to-all-start = ((f32[6,32,128]{2,0,1:T(8,128)}), f32[6,32,128]{2,0,1:T(8,128)S(1)}, u32[]{:S(2)}, u32[]{:S(2)}) async-start(f32[6,32,128]{2,0,1:T(8,128)} %copy.65), calls=%async_computation | async-start | bytes 262144 | tf_op jit(solution)/shard_map/all_to_all | solution.py:145
  136.8 18.9 %all-to-all-start.1 = ((f32[3,32,128]{2,0,1:T(4,128)}), f32[3,32,128]{2,0,1:T(4,128)S(1)}, u32[]{:S(2)}, u32[]{:S(2)}) async-start(f32[3,32,128]{2,0,1:T(4,128)} %copy.68), calls=%async_computation.1 | async-start | bytes 131072 | tf_op jit(solution)/shard_map/all_to_all | solution.py:164
  272.9 9.1 %copy-start = (f32[3,2048]{0,1:T(8,128)S(1)}, f32[3,2048]{0,1:T(8,128)}, u32[]{:S(2)}) copy-start(f32[3,2048]{0,1:T(8,128)} %get-tuple-element.31) | copy-start | bytes 73732
  272.9 7.1 %collective-permute-start.2 = (f32[3,9,1,512]{3,2,1,0:T(1,128)S(1)}, f32[3,9,1,512]{3,2,1,0:T(1,128)S(1)}, u32[]{:S(2)}, u32[]{:S(2)}) collective-permute-start(f32[3,9,1,512]{3,2,1,0:T(1,128)S(1)} %slice.256), channel_id=1, source_target_pairs={{0,1},{1,2},{2,3},{3,4},{4,5},{5,6},{6,7},{8,9},{9,10},{10,11},{11... | collective-permute-start | bytes 165896 | tf_op jit(solution)/shard_map/ppermute | solution.py:13
  277.1 8.4 %copy-start.13 = (f32[8,8,512]{2,1,0:T(8,128)S(1)}, f32[8,8,512]{2,1,0:T(8,128)}, u32[]{:S(2)}) copy-start(f32[8,8,512]{2,1,0:T(8,128)} %param.18) | copy-start | bytes 393220
  280.1 5.4 %collective-permute-start.3 = (f32[3,1,8,512]{3,2,1,0:T(8,128)S(1)}, f32[3,1,8,512]{3,2,1,0:T(8,128)S(1)}, u32[]{:S(2)}, u32[]{:S(2)}) collective-permute-start(f32[3,1,8,512]{3,2,1,0:T(8,128)S(1)} %slice.258), channel_id=1, source_target_pairs={{0,8},{8,16},{16,24},{1,9},{9,17},{17,25},{2,10},{10,18},{18,26},{... | collective-permute-start | bytes 147464 | tf_op jit(solution)/shard_map/ppermute | solution.py:13
where the time goes:
time: 288 us; the launch traced here: 286 us
  other arithmetic  138 us (48%)
  local copies, waits for them, and re-layouts  117 us (41%)
  starting transfers between devices  22.2 us (8%)
  waiting for transfers between devices  8.67 us (3%)
    scatter-add x4, other arithmetic, per_device(): flat_forces = flat_forces.at[:, index].add(quarter)  98.5 us
    gather x7, local copies, waits for them, and re-layouts, per_device(): pieces.append(flat_disp[:, index] + shift_vec)  51.1 us
    scatter-add x1, other arithmetic, per_device(): jnp.zeros((3, slots), jnp.float32).at[:, flat_candidates]  13.1 us
    reshape x2, local copies, waits for them, and re-layouts, per_device(): flat_forces = forces.reshape(3, -1)  12.5 us
    scatter-add x1, local copies, waits for them, and re-layouts, per_device(): flat_forces = flat_forces.at[:, index].add(quarter)  12 us
    reshape x2, local copies, waits for them, and re-layouts, per_device(): flat_disp = extended[3:6].reshape(3, -1)  11.3 us
    ppermute x4, starting transfers between devices, shifted(): return lax.ppermute(array, axis, pairs)  10.6 us
    another operation x3, other arithmetic  9.41 us
  transfers between devices with their start and end apart: 6, of which 4 were waited for; matrix products, arithmetic and copies ran while one was open for 11% of the time, Pallas kernels for 0%

commit v1 on v0

--- a/solution.py
+++ b/solution.py
@@ -142,12 +142,18 @@
     payload = jnp.concatenate([centre_own, area_own], 0)
     width = payload.shape[0]
     outgoing = jnp.zeros((width, slots), jnp.float32).at[:, target].set(payload)
-    arrived = lax.all_to_all(
-        outgoing.reshape(width, devices, capacity),
-        ("gx", "gy"),
-        split_axis=1,
-        concat_axis=1,
-        tiled=True,
+    arrived = jnp.concatenate(
+        lax.all_to_all(
+            jnp.stack(
+                jnp.split(
+                    outgoing.reshape(width, devices, capacity), lax.axis_size(("gx", "gy")), axis=1
+                )
+            ),
+            ("gx", "gy"),
+            0,
+            0,
+        ),
+        axis=1,
     )
     arrived = arrived.reshape(width, slots)
     centre = arrived[0:3]

time: 288 us -> 363 us (1.26)
  local copies, waits for them, and re-layouts: 117 us -> 192 us
    unnamed x58 -> x74, local copies, waits for them, and re-layouts: 5.55 us -> 53.5 us
    gather x7, local copies, waits for them, and re-layouts: 51.1 us -> 63.2 us  [per_device(): pieces.append(flat_disp[:, index] + shift_vec)]
    another operation x1 -> x3, local copies, waits for them, and re-layouts: 0.23 us -> 7.31 us  [the longest x2 7.08 us: per_device(): jnp.stack(jnp.split(outgoing.reshape(width, devices, capacity), lax.axis_...]
    split x0 -> x2, local copies, waits for them, and re-layouts: none -> 4.47 us  [per_device(): jnp.split(outgoing.reshape(width, devices, capacity), lax.axis_size(('gx'...]
    another operation x4, other arithmetic: 5.17 us -> 1.34 us  [element_pass(): jnp.stack([-0.25 * (sign_x * tensor[row][0] + sign_y * tensor[row][1] + s...]
  transfers between devices with their start and end apart: 6 -> 6, of which waited for: 4 -> 4; matrix products, arithmetic and copies ran while one was open for 11% -> 9% of each run, Pallas kernels for 0% -> 0%
where the time goes in v1:
time: 363 us; the launch traced here: 360 us
  local copies, waits for them, and re-layouts  192 us (53%)
  other arithmetic  135 us (37%)
  starting transfers between devices  22.1 us (6%)
  waiting for transfers between devices  8.74 us (2%)
    scatter-add x4, other arithmetic, per_device(): flat_forces = flat_forces.at[:, index].add(quarter)  98.4 us
    gather x7, local copies, waits for them, and re-layouts, per_device(): pieces.append(flat_disp[:, index] + shift_vec)  63.2 us
    unnamed x74, local copies, waits for them, and re-layouts  53.5 us
    scatter-add x1, other arithmetic, per_device(): jnp.zeros((3, slots), jnp.float32).at[:, flat_candidates]  13.1 us
    reshape x2, local copies, waits for them, and re-layouts, per_device(): flat_disp = extended[3:6].reshape(3, -1)  12.5 us
    reshape x2, local copies, waits for them, and re-layouts, per_device(): flat_forces = forces.reshape(3, -1)  12.5 us
    scatter-add x1, local copies, waits for them, and re-layouts, per_device(): flat_forces = flat_forces.at[:, index].add(quarter)  12 us
    ppermute x4, starting transfers between devices, shifted(): return lax.ppermute(array, axis, pairs)  10.6 us
  transfers between devices with their start and end apart: 6, of which 4 were waited for; matrix products, arithmetic and copies ran while one was open for 9% of the time, Pallas kernels for 0%

profile of v1, /device:TPU:12, one launch (start us, length us, event | category | flops | bytes accessed | tf_op | source)
XLA Modules:
  0.0 359.6 jit_solution(2760515532182306431)
XLA Ops:
  2.7 1.9 collective-permute-start
  4.8 9.1 %reduce-window.6 = s32[32,16,128]{2,1,0:T(8,128)S(1)} reduce-window(s32[32,16,128]{2,1,0:T(8,128)S(1)} %fusion.32, s32[]{:T(128)} %constant.89.clone.1), window={size=1x1x128 pad=0_0x0_0x127_0}, to_apply=%region_0.1 | reduce-window | flops 8323072 | bytes 524292 | tf_op jit(solution)/shard_map/reduce-window
  15.4 3.3 collective-permute-start.1
  19.6 3.2 collective-permute-done.1
  24.1 1.9 reshape.125
  26.1 10.6 %copy.145 = f32[3,41553]{0,1:T(8,128)} copy(f32[3,41553]{1,0:T(4,128)S(1)} %reshape.125) | data formatting | bytes 997272 | tf_op jit(solution)/shard_map/reshape | solution.py:131
  36.7 14.6 %gather_fusion.3 = f32[2048,3]{1,0:T(8,128)} fusion(f32[3,41553]{0,1:T(8,128)} %copy.145, s32[2048]{0:T(1024)S(1)} %get-tuple-element.104), kind=kCustom, calls=%fused_computation.3 | custom fusion | bytes 57344 | tf_op jit(solution)/shard_map/gather | solution.py:139
  51.3 1.6 copy.152
  52.8 14.6 %gather_fusion.2 = f32[2048,3]{1,0:T(8,128)} fusion(f32[3,41553]{0,1:T(8,128)} %copy.145, s32[2048]{0:T(1024)S(1)} %get-tuple-element.102), kind=kCustom, calls=%fused_computation.2 | custom fusion | bytes 57344 | tf_op jit(solution)/shard_map/gather | solution.py:139
  67.5 2.3 broadcast_add_fusion
  69.7 1.6 copy.233
  71.3 14.6 %gather_fusion.1 = f32[2048,3]{1,0:T(8,128)} fusion(f32[3,41553]{0,1:T(8,128)} %copy.145, s32[2048]{0:T(1024)S(1)} %get-tuple-element.12), kind=kCustom, calls=%fused_computation.1 | custom fusion | bytes 57344 | tf_op jit(solution)/shard_map/gather | solution.py:139
  85.9 14.6 %gather_fusion = f32[2048,3]{1,0:T(8,128)} fusion(f32[3,41553]{0,1:T(8,128)} %copy.145, s32[2048]{0:T(1024)S(1)} %get-tuple-element.106), kind=kCustom, calls=%fused_computation | custom fusion | bytes 57344 | tf_op jit(solution)/shard_map/gather | solution.py:139
  100.5 1.6 copy.146
  102.1 1.6 copy.148
  105.3 7.4 %scatter_custom_fusion = f32[6,4096]{0,1:T(8,128)} fusion(s32[2048]{0:T(1024)S(1)} %bitcast.245, f32[2048,6]{1,0:T(8,128)} %copy.153, f32[]{:T(128)} %constant.80.clone.1), kind=kCustom, calls=%fused_computation.63 | custom fusion | bytes 98816 | tf_op jit(solution)/shard_map/scatter | solution.py:144
  112.6 2.1 fusion.55
  114.7 2.4 fusion.54
  122.2 1.5 copy.228
  125.2 1.5 copy.208
  129.7 1.5 copy.205
  134.2 1.5 copy.202
  144.6 1.5 copy.226
  147.7 1.5 copy.224
  150.7 1.5 copy.222
  152.2 1.5 copy.221
  156.7 1.5 copy.218
  159.7 1.5 copy.216
  167.9 5.4 %stack.294 = f32[32,6,1,128]{3,0,2,1:T(8,128)} concatenate(f32[1,6,1,128]{3,0,2,1:T(1,128)} %bitcast.263, f32[1,6,1,128]{3,0,2,1:T(1,128)} %bitcast.262, f32[1,6,1,128]{3,0,2,1:T(1,128)} %bitcast.261, f32[1,6,1,128]{3,0,2,1:T(1,128)} %bitcast.260, f32[1,6,1,128]{3,0,2,1:T(1,128)} %bitcast.259, f32[1,6,1,128]{3,0,2,1:T(1,128)} %bitcast.258, f32[1,6,1,128]{3,0,2,1:T(1,128)} %bitcast.257, ...), dimensions={0} | concatenate | bytes 196608 | tf_op jit(solution)/shard_map/stack | solution.py:147
  173.3 1.6 copy.186
  175.0 5.9 %all-to-all-start = ((f32[32,6,1,128]{3,2,1,0:T(1,128)}), f32[32,6,1,128]{3,2,1,0:T(1,128)}, u32[]{:S(2)}, u32[]{:S(2)}) async-start(f32[32,6,1,128]{3,2,1,0:T(1,128)} %copy.186), calls=%async_computation | async-start | bytes 196608 | tf_op jit(solution)/shard_map/all_to_all | solution.py:146
  180.9 4.6 %fusion = f32[3,9,9,513]{3,2,1,0:T(8,128)} fusion(f32[1,8,8,512]{3,2,1,0:T(8,128)S(1)} %get-tuple-element.85, f32[1,8,8,512]{3,2,1,0:T(8,128)S(1)} %get-tuple-element.79, f32[1,8,8,512]{3,2,1,0:T(8,128)S(1)} %get-tuple-element.72, f32[1,8,8,512]{3,2,1,0:T(8,128)S(1)} %get-tuple-element.84, f32[1,8,8,512]{3,2,1,0:T(8,128)S(1)} %get-tuple-element.78, ...), kind=kLoop, calls=%fused_computation.19 | loop fusion | flops 14086467 | bytes 3644364 | tf_op jit(solution)/shard_map/add | solution.py:67
  188.1 5.5 %gather_fusion.4 = f32[2048,6]{1,0:T(8,128)S(1)} fusion(f32[6,4096]{0,1:T(8,128)S(1)} %copy.189, s32[2048]{0:T(1024)S(1)} %get-tuple-element.108), kind=kCustom, calls=%fused_computation.4 | custom fusion | bytes 106496 | tf_op jit(solution)/shard_map/gather | solution.py:163
  193.6 2.3 fusion.56
  195.9 13.1 %scatter_custom_fusion.1 = f32[3,4096]{0,1:T(8,128)S(1)} fusion(s32[2048]{0:T(1024)} %bitcast.249, f32[]{:T(128)} %constant.80.clone.1, f32[2048]{0:T(1024)S(1)} %maximum_multiply_fusion.1, f32[6,2048]{0,1:T(8,128)S(1)} %bitcast.229), kind=kCustom, calls=%fused_computation.58 | custom fusion | flops 18432 | bytes 107008 | tf_op jit(solution)/shard_map/scatter-add | solution.py:169
  210.3 5.6 %all-to-all-start.1 = ((f32[3,32,128]{2,0,1:T(4,128)}), f32[3,32,128]{2,0,1:T(4,128)S(1)}, u32[]{:S(2)}, u32[]{:S(2)}) async-start(f32[3,32,128]{2,0,1:T(4,128)} %copy.191), calls=%async_computation.1 | async-start | bytes 131072 | tf_op jit(solution)/shard_map/all_to_all | solution.py:170
  216.5 1.9 reshape.122
  218.4 10.6 %copy.193 = f32[3,41553]{0,1:T(8,128)} copy(f32[3,41553]{1,0:T(4,128)S(1)} %reshape.122) | data formatting | bytes 997272 | tf_op jit(solution)/shard_map/reshape | solution.py:179
  229.7 5.5 %gather_fusion.5 = f32[2048,3]{1,0:T(8,128)S(1)} fusion(f32[3,4096]{0,1:T(8,128)S(1)} %bitcast.234, s32[2048]{0:T(1024)S(1)} %broadcast_clamp_fusion), kind=kCustom, calls=%fused_computation.5 | custom fusion | bytes 57344 | tf_op jit(solution)/shard_map/gather | solution.py:178
  235.2 24.6 %scatter_custom_fusion.2 = f32[3,41553]{0,1:T(8,128)} fusion(f32[3,41553]{0,1:T(8,128)} %copy.193, s32[2048]{0:T(1024)} %get-tuple-element.107, f32[2048,3]{1,0:T(8,128)S(1)} %gather_fusion.5, f32[]{:T(128)} %constant.81.clone.1), kind=kCustom, calls=%fused_computation.70 | custom fusion | flops 12288 | bytes 523724 | tf_op jit(solution)/shard_map/scatter-add | solution.py:181
  259.8 24.6 %scatter_custom_fusion.3 = f32[3,41553]{0,1:T(8,128)} fusion(f32[3,41553]{0,1:T(8,128)} %scatter_custom_fusion.2, s32[2048]{0:T(1024)} %get-tuple-element.13, f32[2048,3]{1,0:T(8,128)S(1)} %gather_fusion.5, f32[]{:T(128)} %constant.81.clone.1), kind=kCustom, calls=%fused_computation.68 | custom fusion | flops 12288 | bytes 523724 | tf_op jit(solution)/shard_map/scatter-add | solution.py:181
  284.4 24.6 %scatter_custom_fusion.4 = f32[3,41553]{0,1:T(8,128)} fusion(f32[3,41553]{0,1:T(8,128)} %scatter_custom_fusion.3, s32[2048]{0:T(1024)} %get-tuple-element.103, f32[2048,3]{1,0:T(8,128)S(1)} %gather_fusion.5, f32[]{:T(128)} %constant.81.clone.1), kind=kCustom, calls=%fused_computation.66 | custom fusion | flops 12288 | bytes 523724 | tf_op jit(solution)/shard_map/scatter-add | solution.py:181
  309.0 24.6 %scatter_custom_fusion.5 = f32[3,41553]{0,1:T(8,128)} fusion(f32[3,41553]{0,1:T(8,128)} %scatter_custom_fusion.4, s32[2048]{0:T(1024)} %get-tuple-element.105, f32[2048,3]{1,0:T(8,128)S(1)} %gather_fusion.5, f32[]{:T(128)} %constant.81.clone.1), kind=kCustom, calls=%fused_computation.72 | custom fusion | flops 12288 | bytes 523724 | tf_op jit(solution)/shard_map/scatter-add | solution.py:181
  333.6 12.0 %copy.194 = f32[3,41553]{1,0:T(4,128)S(1)} copy(f32[3,41553]{0,1:T(8,128)} %scatter_custom_fusion.5) | data formatting | bytes 997272 | tf_op jit(solution)/shard_map/scatter-add | solution.py:181
  346.2 3.5 collective-permute-start.2
  350.4 2.9 collective-permute-done.2
  353.4 1.9 collective-permute-start.3
  356.4 2.4 collective-permute-done.3
  (109 shorter events, 51.3 us)
Async XLA Ops:
  0.6 4.0 %copy-start.10 = (s32[4,512]{1,0:T(4,128)S(1)}, s32[4,512]{1,0:T(4,128)}, u32[]{:S(2)}) copy-start(s32[4,512]{1,0:T(4,128)} %param.23) | copy-start | bytes 24580
  0.6 4.1 %copy-start.7 = (s32[2048,1]{0,1:T(1,128)S(1)}, s32[2048,1]{0,1:T(1,128)}, u32[]{:S(2)}) copy-start(s32[2048,1]{0,1:T(1,128)} %param.21) | copy-start | bytes 24580
  2.7 12.7 %collective-permute-start = (f32[6,1,8,512]{3,2,1,0:T(8,128)S(1)}, f32[6,1,8,512]{3,2,1,0:T(8,128)S(1)}, u32[]{:S(2)}, u32[]{:S(2)}) collective-permute-start(f32[6,1,8,512]{3,2,1,0:T(8,128)S(1)} %slice.231), channel_id=1, source_target_pairs={{8,0},{16,8},{24,16},{9,1},{17,9},{25,17},{10,2},{18,10},{26,18},{... | collective-permute-start | bytes 294920 | tf_op jit(solution)/shard_map/ppermute | solution.py:13
  4.7 10.0 %copy-start.8 = (s32[2048,1]{0,1:T(1,128)}, s32[2048,1]{0,1:T(1,128)S(1)}, u32[]{:S(2)}) copy-start(s32[2048,1]{0,1:T(1,128)S(1)} %compare_select_fusion.1) | copy-start | bytes 24580
  4.8 10.0 %copy-start.11 = (s32[2048]{0:T(1024)S(1)}, s32[2048]{0:T(1024)}, u32[]{:S(2)}) copy-start(s32[2048]{0:T(1024)} %param.20) | copy-start | bytes 24580
  14.0 4.8 %copy-start.9 = (f32[3,512]{1,0:T(4,128)S(1)}, f32[3,512]{1,0:T(4,128)}, u32[]{:S(2)}) copy-start(f32[3,512]{1,0:T(4,128)} %param.22) | copy-start | bytes 18436
  15.4 7.4 %collective-permute-start.1 = (f32[6,9,1,512]{3,2,1,0:T(1,128)S(1)}, f32[6,9,1,512]{3,2,1,0:T(1,128)S(1)}, u32[]{:S(2)}, u32[]{:S(2)}) collective-permute-start(f32[6,9,1,512]{3,2,1,0:T(1,128)S(1)} %pad_maximum_fusion.3), channel_id=1, source_target_pairs={{1,0},{2,1},{3,2},{4,3},{5,4},{6,5},{7,6},{9,8},{10,9},{11,10},{12... | collective-permute-start | bytes 331784 | tf_op jit(solution)/shard_map/ppermute | solution.py:13
  100.5 3.2 copy-start.12
  100.5 3.2 copy-start.13
  100.5 3.2 copy-start.14
  114.7 2.4 copy-start.1
  117.6 1.0 copy-start.2
  117.6 1.2 copy-start.3
  117.7 1.2 copy-start.5
  122.2 45.0 %copy-start.4 = (f32[6,1,128]{0,2,1:T(8,128)S(1)}, f32[6,1,128]{0,2,1:T(8,128)}, u32[]{:S(2)}) copy-start(f32[6,1,128]{0,2,1:T(8,128)} %get-tuple-element.51) | copy-start | bytes 9220
  175.0 11.5 %all-to-all-start = ((f32[32,6,1,128]{3,2,1,0:T(1,128)}), f32[32,6,1,128]{3,2,1,0:T(1,128)}, u32[]{:S(2)}, u32[]{:S(2)}) async-start(f32[32,6,1,128]{3,2,1,0:T(1,128)} %copy.186), calls=%async_computation | async-start | bytes 196608 | tf_op jit(solution)/shard_map/all_to_all | solution.py:146
  210.3 18.8 %all-to-all-start.1 = ((f32[3,32,128]{2,0,1:T(4,128)}), f32[3,32,128]{2,0,1:T(4,128)S(1)}, u32[]{:S(2)}, u32[]{:S(2)}) async-start(f32[3,32,128]{2,0,1:T(4,128)} %copy.191), calls=%async_computation.1 | async-start | bytes 131072 | tf_op jit(solution)/shard_map/all_to_all | solution.py:170
  346.2 9.1 %copy-start = (f32[3,2048]{0,1:T(8,128)S(1)}, f32[3,2048]{0,1:T(8,128)}, u32[]{:S(2)}) copy-start(f32[3,2048]{0,1:T(8,128)} %get-tuple-element.66) | copy-start | bytes 73732
  346.2 7.1 %collective-permute-start.2 = (f32[3,9,1,512]{3,2,1,0:T(1,128)S(1)}, f32[3,9,1,512]{3,2,1,0:T(1,128)S(1)}, u32[]{:S(2)}, u32[]{:S(2)}) collective-permute-start(f32[3,9,1,512]{3,2,1,0:T(1,128)S(1)} %slice.256), channel_id=1, source_target_pairs={{0,1},{1,2},{2,3},{3,4},{4,5},{5,6},{6,7},{8,9},{9,10},{10,11},{11... | collective-permute-start | bytes 165896 | tf_op jit(solution)/shard_map/ppermute | solution.py:13
  350.4 8.4 %copy-start.6 = (f32[8,8,512]{2,1,0:T(8,128)S(1)}, f32[8,8,512]{2,1,0:T(8,128)}, u32[]{:S(2)}) copy-start(f32[8,8,512]{2,1,0:T(8,128)} %param.18) | copy-start | bytes 393220
  353.4 5.4 %collective-permute-start.3 = (f32[3,1,8,512]{3,2,1,0:T(8,128)S(1)}, f32[3,1,8,512]{3,2,1,0:T(8,128)S(1)}, u32[]{:S(2)}, u32[]{:S(2)}) collective-permute-start(f32[3,1,8,512]{3,2,1,0:T(8,128)S(1)} %slice.258), channel_id=1, source_target_pairs={{0,8},{8,16},{16,24},{1,9},{9,17},{17,25},{2,10},{10,18},{18,26},{... | collective-permute-start | bytes 147464 | tf_op jit(solution)/shard_map/ppermute | solution.py:13
